TPU v7x, 512 devices: a whole 4x8x8 slice. The times are simulated.
512 devices in a mesh: grid: 128 (over y, z, core), slab: 4 (over x).
Axes of the slice: x: 4, y: 8, z: 8, core: 2. Of those that a mesh axis runs over, the one named last changes fastest.
Arguments:
- start_block: float32 [5, 64, 65536], P(None, None, ('grid', 'slab')), may hold values from -6 to 6
- jacobian: float32 [1024, 4, 5, 5, 64], P(('grid', 'slab')), may hold values from -1.5 to 1.5
- block_cols: int32 [1024, 4], P(('grid', 'slab')), may hold values from 0 to 3, as said below
- donor_cell: int32 [65536, 8], P(('grid', 'slab')), may hold values from 0 to 127
- donor_weight: float32 [65536, 8], P(('grid', 'slab')), may hold values from 0.05 to 0.25
- fringe_dest: int32 [65536, 1], P(('grid', 'slab')), may hold values from 0 to 127; in each aligned block of 128 rows (0 to 127, 128 to 255, ...) at most 2 rows name the same one
- recv_cell: int32 [65536], P(('grid', 'slab')), may hold values from 0 to 127
Outputs:
- basis: float32 [2, 5, 64, 65536], P(None, None, None, ('grid', 'slab'))
- projection: float32 [64, 128], replicated
- factor: float32 [128, 128], replicated
Inputs may be any that keep to these rules, and one draw needn't show every extreme that they name: `block_cols`: the first entry of each block row is its own block (its index within the device plus 1); the first block row of every device lists block 0 and the last lists block 3 as second entry. `fringe_dest`: the 128 fringe cells of one device name any one grid index at most 2 times.
All inputs are finite; a program needn't handle non-finite values.
Results may differ from a plain program's by a relative error of at most 0.0003.
Values sent between devices are 32-bit elements; how exact they have to be, the bound alone decides.
A program may use at most 64 MiB of HBM per device.

v0:
```python
import jax
import jax.numpy as jnp
from jax import lax
from jax.sharding import PartitionSpec as P


def extended(shard, sides, width):
    for axis, dim in sides:
        size, length = (lax.axis_size(axis), shard.shape[dim])
        up = [(i, (i + 1) % size) for i in range(size - 1)]
        down = [(j, i) for i, j in up]
        last = lax.slice_in_dim(shard, length - width, length, axis=dim)
        leading = lax.slice_in_dim(shard, 0, width, axis=dim)
        before = lax.ppermute(last, axis, up)
        after = lax.ppermute(leading, axis, down)
        shard = jnp.concatenate([before, shard, after], axis=dim)
    return shard


def apply_blocks(field, jacobian, block_cols):
    var_count, rhs_count, cell_count = field.shape
    block_count, neighbors, _, _, block_len = jacobian.shape
    padded = extended(field, (("slab", 2),), block_len)
    padded = padded.reshape(var_count, rhs_count, block_count + 2, block_len)
    result = field
    for column in range(neighbors):
        picked = jnp.take(padded, block_cols[:, column], axis=2)
        term = jnp.einsum(
            "iabc,bric->aric", jacobian[:, column], picked, precision=lax.Precision.HIGHEST
        )
        result = result + term.reshape(var_count, rhs_count, cell_count)
    return result


def fringe_add(local_part, received):
    values, scatter_mat = received
    width = values.shape[0]
    flat = values.reshape(width, -1)
    return local_part + jnp.dot(flat, scatter_mat, precision=lax.Precision.HIGHEST).reshape(
        local_part.shape
    )


def cell_matrix(slot_cells, cell_count):
    cell_ids = jnp.arange(cell_count, dtype=jnp.int32)
    return (slot_cells.reshape(-1)[:, None] == cell_ids[None, :]).astype(jnp.float32)


def project_out(start_block, stacked, total_rows):
    local_proj = (
        jnp.einsum("vrc,jvsc->rjs", start_block, stacked, precision=lax.Precision.HIGHEST)
        / total_rows
    )
    return lax.psum(local_proj, ("grid", "slab"))


def upper_factor(gram):
    return jnp.linalg.cholesky(gram).T


def shards(start_block, jacobian, block_cols, donor_cell, donor_weight, fringe_dest, recv_cell):
    var_count, rhs_count, cell_count = start_block.shape
    grid_count = lax.axis_size("grid")
    device_count = grid_count * lax.axis_size("slab")
    fringe_rows = donor_cell.shape[0]
    capacity = max(2, 2 * fringe_rows // grid_count)
    slot_count = grid_count * capacity
    total_rows = var_count * cell_count * device_count
    width = var_count * rhs_count
    targets = fringe_dest[:, 0]
    row_ids = jnp.arange(fringe_rows, dtype=jnp.int32)
    same_target = targets[:, None] == targets[None, :]
    earlier = row_ids[None, :] < row_ids[:, None]
    slot_index = jnp.sum((same_target & earlier).astype(jnp.int32), axis=1)
    position = targets * capacity + slot_index
    slot_ids = jnp.arange(slot_count, dtype=jnp.int32)
    place_bool = position[:, None] == slot_ids[None, :]
    place = place_bool.astype(jnp.float32)
    cell_ids = jnp.arange(cell_count, dtype=jnp.int32)
    donor_onehot = (donor_cell[:, :, None] == cell_ids[None, None, :]).astype(jnp.float32)
    weight_mat = jnp.sum(donor_onehot * donor_weight[:, :, None], axis=1)
    send_mat = jnp.dot(weight_mat.T, place, precision=lax.Precision.HIGHEST)
    slot_cells = jnp.sum(jnp.where(place_bool, recv_cell[:, None] + 1, 0), axis=0) - 1
    slot_cells = slot_cells.reshape(1, grid_count, capacity)

    def outgoing(field):
        sent = jnp.dot(field.reshape(width, cell_count), send_mat, precision=lax.Precision.HIGHEST)
        return sent.reshape(width, grid_count, capacity)

    local_first = apply_blocks(start_block, jacobian, block_cols)
    arrived, arrived_cells = (
        lax.all_to_all(outgoing(start_block), "grid", split_axis=1, concat_axis=1, tiled=True),
        lax.all_to_all(slot_cells, "grid", split_axis=1, concat_axis=1, tiled=True),
    )
    scatter_mat = cell_matrix(arrived_cells, cell_count)
    first = fringe_add(local_first, (arrived, scatter_mat))
    local_second = apply_blocks(first, jacobian, block_cols)
    arrived_two = lax.all_to_all(outgoing(first), "grid", split_axis=1, concat_axis=1, tiled=True)
    second = fringe_add(local_second, (arrived_two, scatter_mat))
    stacked = jnp.stack([first, second])
    projection = project_out(start_block, stacked, total_rows)
    proj_mat = projection.reshape(rhs_count, 2 * rhs_count)
    projected = stacked - jnp.einsum(
        "vrc,rjs->jvsc", start_block, projection, precision=lax.Precision.HIGHEST
    )
    local_gram = (
        jnp.einsum("jvrc,kvsc->jrks", projected, projected, precision=lax.Precision.HIGHEST)
        / total_rows
    )
    gram = lax.psum(local_gram, ("grid", "slab")).reshape(2 * rhs_count, 2 * rhs_count)
    factor = upper_factor(gram)
    columns = jnp.transpose(projected, (0, 2, 1, 3)).reshape(2 * rhs_count, var_count * cell_count)
    solved = lax.linalg.triangular_solve(factor.T, columns, left_side=True, lower=True)
    basis = jnp.transpose(solved.reshape(2, rhs_count, var_count, cell_count), (0, 2, 1, 3))
    return (basis, proj_mat, factor)


def solution(mesh):
    in_specs = (
        P(None, None, ("grid", "slab")),
        P(("grid", "slab"), None, None, None, None),
        P(("grid", "slab"), None),
        P(("grid", "slab"), None),
        P(("grid", "slab"), None),
        P(("grid", "slab"), None),
        P(("grid", "slab")),
    )
    out_specs = (P(None, None, None, ("grid", "slab")), P(), P())
    return jax.shard_map(shards, mesh=mesh, in_specs=in_specs, out_specs=out_specs, check_vma=False)
```

profile of v0, /device:TPU:1, one launch (start us, length us, event | category | flops | bytes accessed | tf_op | source)
XLA Modules:
  0.0 514.0 jit_solution(18358035796766674069)
XLA Ops:
  7.2 1.1 fusion.43
  8.3 4.6 collective-permute-start
  12.9 1.4 collective-permute-start.1
  15.3 0.8 sub.10
  16.1 18.0 %all-to-all-start.1 = ((s32[1,128,2]{2,0,1:T(1,128)}), s32[1,128,2]{2,0,1:T(1,128)S(1)}, u32[]{:S(2)}, u32[]{:S(2)}) async-start(s32[1,128,2]{2,0,1:T(1,128)} %bitcast.21), calls=%async_computation.1 | async-start | bytes 131072 | tf_op jit(solution)/shard_map/all_to_all | solution.py:93
  34.5 0.7 copy-done.8
  38.6 1.0 reshape.108
  39.5 0.7 copy.189
  40.3 5.3 %all-to-all-done.1 = s32[1,128,2]{2,0,1:T(1,128)S(1)} async-done(((s32[1,128,2]{2,0,1:T(1,128)}), s32[1,128,2]{2,0,1:T(1,128)S(1)}, u32[]{:S(2)}, u32[]{:S(2)}) %all-to-all-start.1) | async-done | bytes 1056 | tf_op jit(solution)/shard_map/all_to_all | solution.py:93
  45.5 8.9 %all-to-all-start = ((f32[320,128,2]{0,2,1:T(2,128)}), f32[320,128,2]{0,2,1:T(2,128)}, u32[]{:S(2)}, u32[]{:S(2)}) async-start(f32[320,128,2]{0,2,1:T(2,128)} %reshape.108), calls=%async_computation | async-start | bytes 786432 | tf_op jit(solution)/shard_map/all_to_all | solution.py:92
  54.9 0.8 reduce.17
  55.9 1.2 pad_maximum_fusion
  57.1 1.2 reshape.102
  58.2 1.2 copy.156
  59.4 1.3 gather_fusion
  60.7 1.1 select_bitcast_fusion.7
  61.8 1.0 copy.158
  62.8 2.0 fusion.21
  64.8 0.8 copy.159
  65.6 1.3 gather_fusion.1
  66.9 1.1 select_bitcast_fusion.6
  68.0 1.0 copy.162
  69.0 2.0 fusion.17
  71.0 0.8 copy.163
  71.9 1.3 gather_fusion.2
  73.1 1.1 select_bitcast_fusion.5
  74.2 1.0 copy.166
  75.2 2.0 fusion.13
  77.3 0.8 copy.167
  79.0 1.0 fusion.9
  80.0 0.8 copy.171
  80.8 1.4 dot_general.65
  82.2 1.9 convolution_add_fusion.1
  84.2 4.3 collective-permute-start.2
  88.5 1.3 collective-permute-start.3
  90.3 0.9 copy.191
  91.2 14.4 %all-to-all-start.2 = ((f32[320,128,2]{0,2,1:T(2,128)}), f32[320,128,2]{0,2,1:T(2,128)}, u32[]{:S(2)}, u32[]{:S(2)}) async-start(f32[320,128,2]{0,2,1:T(2,128)} %copy.191), calls=%async_computation.2 | async-start | bytes 786432 | tf_op jit(solution)/shard_map/all_to_all | solution.py:98
  106.1 1.1 reshape.109
  107.2 1.2 copy.177
  109.0 1.3 gather_fusion.5
  110.3 1.3 gather_fusion.6
  111.5 1.3 gather_fusion.7
  113.2 1.0 fusion.19
  114.3 0.8 copy-done.3
  115.5 1.0 fusion.15
  116.6 0.8 copy-done.2
  117.7 1.0 fusion.11
  118.9 0.8 copy-done.1
  120.0 1.0 fusion.7
  121.2 0.9 all-to-all-done.2
  122.1 1.4 dot_general.74
  123.5 0.7 fusion.1
  124.7 99.5 %psum.14 = f32[64,2,64]{0,2,1:T(8,128)S(1)} all-reduce(f32[64,2,64]{0,2,1:T(8,128)S(1)} %fusion.4), channel_id=1, replica_groups=mesh['grid'=128,'slab'=4] {'grid','slab'}, use_global_device_ids=true, to_apply=%region_3.5 | all-reduce | flops 8192 | bytes 65536 | tf_op jit(solution)/shard_map/psum | solution.py:54
  224.7 0.7 fusion.2
  225.5 0.8 reshape.115
  226.7 0.7 copy.198
  227.4 253.8 %all-reduce.2.cloned.1.call-done = f32[128,128]{0,1:T(8,128)} async-done(((f32[128,128]{0,1:T(8,128)}), f32[128,128]{0,1:T(8,128)}) %all-reduce.2.cloned.1.call-update) | async-done | bytes 65552 | tf_op jit(solution)/shard_map/psum | solution.py:110
  481.2 1.0 copy.194
  482.2 11.7 %cholesky.16 = f32[128,128]{1,0:T(8,128)S(1)} custom-call(f32[128,128]{1,0:T(8,128)S(1)} %fusion.34), custom_call_target="Cholesky" | custom-call | tf_op jit(solution)/shard_map/jit(cholesky)/cholesky | solution.py:58
  494.0 0.6 compare_reduce_fusion
  494.6 0.7 fusion.39
  495.3 9.8 %custom-call.6 = f32[1,128,128]{1,2,0:T(8,128)S(1)} custom-call(f32[1,128,128]{2,1,0:T(8,128)S(1)} %get-tuple-element.32), custom_call_target="InvertDiagBlocksLowerTriangular" | custom-call | tf_op jit(solution)/shard_map/triangular_solve | solution.py:113
  505.2 0.7 copy.199
  506.0 1.2 convolution_bitcast_fusion
  (82 shorter events, 11.2 us)
Async XLA Ops:
  8.3 47.6 %collective-permute-start = (f32[5,64,64]{2,1,0:T(8,128)S(1)}, f32[5,64,64]{2,1,0:T(8,128)}, u32[]{:S(2)}, u32[]{:S(2)}) collective-permute-start(f32[5,64,64]{2,1,0:T(8,128)S(1)} %get-tuple-element.25), channel_id=1, source_target_pairs={{0,1},{1,2},{2,3},{4,5},{5,6},{6,7},{8,9},{9,10},{10,11},{12,13},{... | collective-permute-start | bytes 245768 | tf_op jit(solution)/shard_map/ppermute | solution.py:14
  12.9 1.4 copy-start.10
  12.9 43.0 %collective-permute-start.1 = (f32[5,64,64]{2,1,0:T(8,128)S(1)}, f32[5,64,64]{2,1,0:T(8,128)}, u32[]{:S(2)}, u32[]{:S(2)}) collective-permute-start(f32[5,64,64]{2,1,0:T(8,128)S(1)} %get-tuple-element.26), channel_id=1, source_target_pairs={{1,0},{2,1},{3,2},{5,4},{6,5},{7,6},{9,8},{10,9},{11,10},{13,12},{... | collective-permute-start | bytes 245768 | tf_op jit(solution)/shard_map/ppermute | solution.py:15
  14.5 0.7 copy-start.11
  15.3 19.1 %copy-start.6 = (f32[2,4,5,5,64]{4,1,3,2,0:T(4,128)S(1)}, f32[2,4,5,5,64]{4,1,3,2,0:T(4,128)}, u32[]{:S(2)}) copy-start(f32[2,4,5,5,64]{4,1,3,2,0:T(4,128)} %param.10) | copy-start | bytes 153604
  16.1 18.0 %copy-start.7 = (s32[2,4]{1,0:T(2,128)S(1)}, s32[2,4]{1,0:T(2,128)}, u32[]{:S(2)}) copy-start(s32[2,4]{1,0:T(2,128)} %param.11) | copy-start | bytes 100
  16.1 29.5 %all-to-all-start.1 = ((s32[1,128,2]{2,0,1:T(1,128)}), s32[1,128,2]{2,0,1:T(1,128)S(1)}, u32[]{:S(2)}, u32[]{:S(2)}) async-start(s32[1,128,2]{2,0,1:T(1,128)} %bitcast.21), calls=%async_computation.1 | async-start | bytes 131072 | tf_op jit(solution)/shard_map/all_to_all | solution.py:93
  34.5 0.7 copy-start.8
  35.2 0.7 copy-start.9
  36.0 0.9 copy-start
  45.5 35.3 %all-to-all-start = ((f32[320,128,2]{0,2,1:T(2,128)}), f32[320,128,2]{0,2,1:T(2,128)}, u32[]{:S(2)}, u32[]{:S(2)}) async-start(f32[320,128,2]{0,2,1:T(2,128)} %reshape.108), calls=%async_computation | async-start | bytes 786432 | tf_op jit(solution)/shard_map/all_to_all | solution.py:92
  84.1 5.7 %copy-start.4 = (f32[256,128]{1,0:T(8,128)S(1)}, f32[256,128]{1,0:T(8,128)}, u32[]{:S(2)}) copy-start(f32[256,128]{1,0:T(8,128)} %copy.189) | copy-start | bytes 393220
  84.2 21.6 %collective-permute-start.2 = (f32[5,64,64]{2,1,0:T(8,128)S(1)}, f32[5,64,64]{2,1,0:T(8,128)S(1)}, u32[]{:S(2)}, u32[]{:S(2)}) collective-permute-start(f32[5,64,64]{2,1,0:T(8,128)S(1)} %get-tuple-element.23), channel_id=1, source_target_pairs={{0,1},{1,2},{2,3},{4,5},{5,6},{6,7},{8,9},{9,10},{10,11},{12,13},{... | collective-permute-start | bytes 245768 | tf_op jit(solution)/shard_map/ppermute | solution.py:14
  88.5 17.4 %collective-permute-start.3 = (f32[5,64,64]{2,1,0:T(8,128)S(1)}, f32[5,64,64]{2,1,0:T(8,128)S(1)}, u32[]{:S(2)}, u32[]{:S(2)}) collective-permute-start(f32[5,64,64]{2,1,0:T(8,128)S(1)} %get-tuple-element.24), channel_id=1, source_target_pairs={{1,0},{2,1},{3,2},{5,4},{6,5},{7,6},{9,8},{10,9},{11,10},{13,12},{... | collective-permute-start | bytes 245768 | tf_op jit(solution)/shard_map/ppermute | solution.py:15
  91.2 30.9 %all-to-all-start.2 = ((f32[320,128,2]{0,2,1:T(2,128)}), f32[320,128,2]{0,2,1:T(2,128)}, u32[]{:S(2)}, u32[]{:S(2)}) async-start(f32[320,128,2]{0,2,1:T(2,128)} %copy.191), calls=%async_computation.2 | async-start | bytes 786432 | tf_op jit(solution)/shard_map/all_to_all | solution.py:98
  105.6 375.6 %all-reduce.2.cloned.1.call-start = ((), (), s32[]{:S(2)}) async-start(), calls=%async_computation.3 | async-start | bytes 131072 | tf_op jit(solution)/shard_map/psum | solution.py:110
  114.1 1.0 copy-start.3
  116.4 1.0 copy-start.2
  118.7 1.0 copy-start.1
  481.2 1.0 copy-start.5
Sparse Core Ops, SparseCore 0:
  226.4 254.7 all-reduce.1
where the time goes:
time: 515 us; the launch traced here: 514 us
  waiting for transfers between devices  260 us (50%)
  blocking collectives  99.5 us (19%)
  starting transfers between devices  53.1 us (10%)
  local copies, waits for them, and re-layouts  39.8 us (8%)
  other arithmetic  29.4 us (6%)
  matrix products  17.5 us (3%)
  between operations  14.7 us (3%)
    psum x1, waiting for transfers between devices, shards(): lax.psum(local_gram, ('grid', 'slab')).reshape(2 * rhs_count, 2 * rhs_count)  254 us
    psum x1, blocking collectives, project_out(): return lax.psum(local_proj, ('grid', 'slab'))  99.5 us
    all_to_all x1, starting transfers between devices, shards(): lax.all_to_all(slot_cells, 'grid', split_axis=1, concat_axis=1, tiled=True)  18 us
    all_to_all x1, starting transfers between devices, shards(): lax.all_to_all(outgoing(first), 'grid', split_axis=1, concat_axis=1, tile...  14.4 us
    another operation x3, other arithmetic, upper_factor(): return jnp.linalg.cholesky(gram).T  12.4 us
    dot_general x8, matrix products, apply_blocks(): jnp.einsum('iabc,bric->aric', jacobian[:, column], picked, precision=lax....  11 us
  transfers between devices with their start and end apart: 8, of which 3 were waited for; matrix products, arithmetic and copies ran while one was open for 9% of the time, Pallas kernels for 0%

commit v1 on v0

v1 whole, which is shorter than its diff:
```python
import functools

import jax
import jax.numpy as jnp
from jax import lax
from jax.experimental import pallas as pl
from jax.experimental.pallas import tpu as pltpu
from jax.sharding import PartitionSpec as P

MESH = pl.DeviceIdType.MESH
F32 = jnp.float32
BF16 = jnp.bfloat16
NT = (((1,), (1,)), ((), ()))
NN = (((1,), (0,)), ((), ()))
TN = (((0,), (0,)), ((), ()))
LANES = 128
HALF = 64
PACK = 32


def halves(x):
    high = x.astype(BF16)
    return high, (x - high.astype(F32)).astype(BF16)


def dot1(a, b, dims):
    return lax.dot_general(a, b, dims, preferred_element_type=F32)


def dot3(a, b, dims):
    ah, al = halves(a)
    bh, bl = halves(b)
    return dot1(ah, bh, dims) + (dot1(ah, bl, dims) + dot1(al, bh, dims))


def lane_ids(shape):
    return lax.broadcasted_iota(jnp.int32, shape, len(shape) - 1)


def row_ids(shape):
    return lax.broadcasted_iota(jnp.int32, shape, len(shape) - 2)


def swap_halves(x):
    return pltpu.roll(x, HALF, x.ndim - 1)


def wide(field):
    return jnp.concatenate([field[v] for v in range(field.shape[0])], axis=1)


def split_rows(packed):
    return jnp.concatenate([packed[:, :HALF], packed[:, HALF:]], axis=0)


def eliminate(gram):
    size = gram.shape[0]
    eye = (row_ids((size, size)) == lane_ids((size, size))).astype(F32)
    work = jnp.concatenate([gram, eye], axis=1)
    blocks = [work[8 * i:8 * i + 8] for i in range(size // 8)]
    sub = row_ids((8, LANES))
    done = []
    for kb in range(len(blocks)):
        cols = {
            i: [jnp.broadcast_to(blocks[i][:, 8 * kb + t:8 * kb + t + 1], (8, LANES)) for t in range(8)]
            for i in range(kb, len(blocks))
        }
        pivots = jnp.ones((8, LANES), F32)
        for t in range(8):
            row = jnp.broadcast_to(blocks[kb][t:t + 1], (8, LANES))
            heads = [jnp.broadcast_to(cols[kb][u][t:t + 1], (8, LANES)) for u in range(t, 8)]
            inverse = 1.0 / heads[0]
            pivots = jnp.where(sub == t, heads[0], pivots)
            for i in range(kb, len(blocks)):
                ratio = cols[i][t] * inverse
                if i == kb:
                    ratio = jnp.where(sub > t, ratio, 0.0)
                for u in range(t + 1, 8):
                    cols[i][u] = cols[i][u] - ratio * heads[u - t]
                blocks[i] = blocks[i] - ratio * row
        done.append(blocks[kb] * lax.rsqrt(pivots))
    both = jnp.concatenate(done, axis=0)
    upper = jnp.where(row_ids((size, size)) <= lane_ids((size, size)), both[:, :size], 0.0)
    return upper, both[:, size:]


class Sizes:
    def __init__(self, grid, slab, low, total_rows):
        self.grid, self.slab, self.low = grid, slab, low
        self.high = grid // low
        self.first = self.high * slab
        self.share = PACK // self.first
        self.total_rows = total_rows


def kernel(
    sz, cols_ref, x_ref, jac_ref, cell_ref, weight_ref, dest_ref, recv_ref,
    basis_ref, proj_ref, factor_ref,
    w1_ref, w2_ref, jeff_ref, send1, send2, got1, got2, place_ref, scatter_ref,
    edge_out1, edge_in1, edge_out2, edge_in2,
    part_e, a_e, mid_e, b_e, sum_e, all_e,
    part_l, a_l, mid_l, b_l, sum_l, all_l,
    fr_send, fr_recv, ed_send, ed_recv, red_send, red_recv,
):
    var_count = x_ref.shape[0]
    g = lax.axis_index("grid")
    s = lax.axis_index("slab")
    hi = lax.div(g, sz.low)
    lo = lax.rem(g, sz.low)
    me1 = hi * sz.slab + s

    def first_peer(i):
        q = lax.rem(me1 + i, sz.first)
        return q, (lax.div(q, sz.slab) * sz.low + lo, lax.rem(q, sz.slab))

    def second_peer(i):
        q = lax.rem(lo + i, sz.low)
        return q, (hi * sz.low + q, s)

    if sz.grid < LANES:
        got1[...] = jnp.zeros_like(got1)
        got2[...] = jnp.zeros_like(got2)

    barrier = pltpu.get_barrier_semaphore()

    def greet_grid(i, carry):
        pl.semaphore_signal(barrier, inc=1, device_id=(lax.rem(g + i, sz.grid), s), device_id_type=MESH)
        return carry

    lax.fori_loop(1, sz.grid, greet_grid, 0)

    def greet_slab(i, carry):
        peer_s = lax.rem(s + 1 + lax.div(i, sz.high), sz.slab)
        peer_h = lax.rem(i, sz.high)
        pl.semaphore_signal(barrier, inc=1, device_id=(peer_h * sz.low + lo, peer_s), device_id_type=MESH)
        return carry

    lax.fori_loop(0, (sz.slab - 1) * sz.high, greet_slab, 0)

    rows = cell_ref.shape[0]
    lanes = lane_ids((rows, LANES))
    weight_mat = jnp.zeros((rows, LANES), F32)
    for t in range(cell_ref.shape[1]):
        weight_mat += jnp.where(cell_ref[:, t:t + 1] == lanes, weight_ref[:, t:t + 1], 0.0)
    named = dest_ref[...] == lanes
    earlier = (lane_ids((rows, rows)) < row_ids((rows, rows))).astype(BF16)
    rank = dot1(earlier, named.astype(BF16), NN)
    slots = jnp.concatenate(
        [jnp.where(named, (rank == float(j)).astype(F32), 0.0) for j in range(2)], axis=1
    ).astype(BF16)
    on_diagonal = row_ids((rows, rows)) == lane_ids((rows, rows))
    recv_col = jnp.sum(jnp.where(on_diagonal, recv_ref[...].astype(F32) + 1.0, 0.0), axis=1, keepdims=True)
    table = jnp.concatenate([weight_mat, jnp.broadcast_to(recv_col, (rows, LANES))], axis=1)
    th, tl = halves(table)
    placed = dot1(slots, th, TN) + dot1(slots, tl, TN)
    place_ref[...] = jnp.concatenate([placed[:LANES, :LANES], placed[LANES:, :LANES]], axis=1)
    cell_row = jnp.where(lanes < HALF, placed[:LANES, LANES:], placed[LANES:, LANES:])

    def fill_fringe(field_ref, out_ref):
        zero = jnp.zeros((HALF, LANES), F32)
        blocks = []
        for v in range(var_count):
            x = field_ref[v]
            blocks += [jnp.concatenate([x, zero], axis=1), jnp.concatenate([zero, x], axis=1)]
        out = dot3(place_ref[...], jnp.concatenate(blocks, axis=0), NT)
        for v in range(var_count):
            out_ref[:, v, :] = out[:, LANES * v:LANES * (v + 1)]

    def fill_edges(field_ref, out_ref):
        low_half = lane_ids((PACK, LANES)) < HALF
        for v in range(var_count):
            top, bottom = field_ref[v, :PACK, :], field_ref[v, PACK:, :]
            out_ref[0, v] = jnp.where(low_half, swap_halves(top), bottom)
            out_ref[1, v] = jnp.where(low_half, top, swap_halves(bottom))

    def start_edges(out_ref, in_ref, which):
        for side, step in ((0, 1), (1, sz.slab - 1)):
            pltpu.make_async_remote_copy(
                src_ref=out_ref.at[side], dst_ref=in_ref.at[side],
                send_sem=ed_send.at[2 * which + side], recv_sem=ed_recv.at[2 * which + side],
                device_id=(g, lax.rem(s + step, sz.slab)), device_id_type=MESH,
            ).start()

    def wait_edges(ref, sems, which):
        for side in range(2):
            pltpu.make_async_copy(ref.at[side], ref.at[side], sems.at[2 * which + side]).wait()

    def start_fringe(out_ref, in_ref, which):
        def body(i, carry):
            p = lax.rem(g + i * 37, sz.grid)
            pltpu.make_async_remote_copy(
                src_ref=out_ref.at[p], dst_ref=in_ref.at[g],
                send_sem=fr_send.at[which], recv_sem=fr_recv.at[which],
                device_id=(p, s), device_id_type=MESH,
            ).start()
            return carry

        lax.fori_loop(1, sz.grid, body, 0)

    def wait_many(ref, count, sem):
        pltpu.make_async_copy(ref.at[pl.ds(0, count)], ref.at[pl.ds(0, count)], sem).wait()

    def own_terms(field_ref, out_ref):
        low_half = lane_ids((HALF, LANES)) < HALF
        for v in range(var_count):
            x = field_ref[v]
            flipped = swap_halves(x)
            left, right = jnp.where(low_half, x, flipped), jnp.where(low_half, flipped, x)
            for a in range(var_count):
                term = jeff_ref[1, a, v:v + 1, :] * left + jeff_ref[2, a, v:v + 1, :] * right
                base = field_ref[a] if v == 0 else out_ref[a]
                out_ref[a] = base + term

    def edge_terms(in_ref, out_ref):
        low_half = lane_ids((PACK, LANES)) < HALF
        for v in range(var_count):
            spread = []
            for side in range(2):
                packed = in_ref[side, v]
                flipped = swap_halves(packed)
                spread.append(jnp.concatenate(
                    [jnp.where(low_half, packed, flipped), jnp.where(low_half, flipped, packed)], axis=0))
            for a in range(var_count):
                term = jeff_ref[0, a, v:v + 1, :] * spread[0] + jeff_ref[3, a, v:v + 1, :] * spread[1]
                out_ref[a] = out_ref[a] + term

    def fringe_terms(in_ref, out_ref):
        left = []
        for v in range(var_count):
            turned = jnp.transpose(in_ref[:, v, :])
            left.append(jnp.concatenate([turned[:HALF], turned[HALF:]], axis=1))
        lh, ll = halves(jnp.concatenate(left, axis=0))
        scatter = scatter_ref[...]
        total = dot1(lh, scatter, NN) + dot1(ll, scatter, NN)
        for v in range(var_count):
            out_ref[v] = out_ref[v] + total[HALF * v:HALF * (v + 1)]

    fill_edges(x_ref, edge_out1)
    fill_fringe(x_ref, send1)
    send1[:, var_count, :] = cell_row
    got1[g] = send1[g]
    pl.semaphore_wait(barrier, sz.grid - 1 + (sz.slab - 1) * sz.high)
    start_edges(edge_out1, edge_in1, 0)
    start_fringe(send1, got1, 0)

    side_on = [(s > 0).astype(F32), F32(1.0), F32(1.0), (s < sz.slab - 1).astype(F32)]
    low_lane = lane_ids((1, LANES)) < HALF
    for a in range(var_count):
        sums = [jnp.zeros((var_count, LANES), F32) for _ in range(4)]
        for k in range(jac_ref.shape[1]):
            both = jnp.concatenate([jac_ref[0, k, a], jac_ref[1, k, a]], axis=1)
            for j in range(4):
                picks = [jnp.where(cols_ref[i, k] == j, side_on[j], F32(0.0)) for i in range(2)]
                sums[j] += jnp.where(low_lane, picks[0], picks[1]) * both
        for j in range(4):
            jeff_ref[j, a, 0:var_count, :] = sums[j]

    own_terms(x_ref, w1_ref)
    wait_edges(edge_in1, ed_recv, 0)
    edge_terms(edge_in1, w1_ref)
    wait_many(got1, sz.grid - 1, fr_recv.at[0])
    cells = got1[:, var_count, :]
    ids = (lanes + 1).astype(F32)
    scatter_ref[...] = jnp.concatenate(
        [(cells[:, j * HALF:j * HALF + 1] == ids).astype(F32) for j in range(2)], axis=0
    ).astype(BF16)
    fringe_terms(got1, w1_ref)

    fill_edges(w1_ref, edge_out2)
    start_edges(edge_out2, edge_in2, 1)
    fill_fringe(w1_ref, send2)
    got2[g] = send2[g]
    start_fringe(send2, got2, 1)

    def reduce_start(part, a_buf, which):
        mine = me1 * sz.share
        a_buf[me1] = part[pl.ds(mine, sz.share)]

        def body(i, carry):
            q, peer = first_peer(i)
            pltpu.make_async_remote_copy(
                src_ref=part.at[pl.ds(q * sz.share, sz.share)], dst_ref=a_buf.at[me1],
                send_sem=red_send.at[which], recv_sem=red_recv.at[which],
                device_id=peer, device_id_type=MESH,
            ).start()
            return carry

        lax.fori_loop(1, sz.first, body, 0)

    def reduce_middle(a_buf, mid, b_buf, which):
        wait_many(a_buf, sz.first - 1, red_recv.at[which])
        value = a_buf[0]
        for i in range(1, sz.first):
            value = value + a_buf[i]
        mid[...] = value
        b_buf[lo] = value

        def body(i, carry):
            _, peer = second_peer(i)
            pltpu.make_async_remote_copy(
                src_ref=mid, dst_ref=b_buf.at[lo],
                send_sem=red_send.at[which + 1], recv_sem=red_recv.at[which + 1],
                device_id=peer, device_id_type=MESH,
            ).start()
            return carry

        lax.fori_loop(1, sz.low, body, 0)

    def reduce_last(b_buf, sum_buf, all_buf, which):
        wait_many(b_buf, sz.low - 1, red_recv.at[which + 1])
        value = b_buf[0]
        for i in range(1, sz.low):
            value = value + b_buf[i]
        sum_buf[...] = value
        all_buf[me1] = value

        def body(i, carry):
            _, peer = first_peer(i)
            pltpu.make_async_remote_copy(
                src_ref=sum_buf, dst_ref=all_buf.at[me1],
                send_sem=red_send.at[which + 2], recv_sem=red_recv.at[which + 2],
                device_id=peer, device_id_type=MESH,
            ).start()
            return carry

        lax.fori_loop(1, sz.first, body, 0)

    def reduced(all_buf, which):
        wait_many(all_buf, sz.first - 1, red_recv.at[which + 2])
        scale = 1.0 / sz.total_rows
        return [all_buf[:, :, t, :].reshape(PACK, LANES) * scale for t in range(3)]

    low_half = lane_ids((PACK, LANES)) < HALF
    wide_x = wide(x_ref)
    wide_1 = wide(w1_ref)
    pair = jnp.concatenate([wide_x, wide_1], axis=0)
    early = dot3(pair, pair, NT)
    part_e[:, 0, :] = early[:PACK]
    part_e[:, 1, :] = early[PACK:HALF]
    part_e[:, 2, :] = jnp.where(low_half, swap_halves(early[HALF:HALF + PACK]), early[HALF + PACK:])
    reduce_start(part_e, a_e, 0)
    own_terms(w1_ref, w2_ref)
    reduce_middle(a_e, mid_e, b_e, 0)
    wait_edges(edge_in2, ed_recv, 1)
    edge_terms(edge_in2, w2_ref)
    reduce_last(b_e, sum_e, all_e, 0)
    wait_many(got2, sz.grid - 1, fr_recv.at[1])
    fringe_terms(got2, w2_ref)

    wide_2 = wide(w2_ref)
    late = dot3(jnp.concatenate([wide_x, wide_1, wide_2], axis=0), wide_2, NT)
    for t in range(3):
        block = late[HALF * t:HALF * (t + 1)]
        part_l[:, t, :] = jnp.concatenate([block[:PACK], block[PACK:]], axis=1)
    reduce_start(part_l, a_l, 3)

    top, bottom, third = reduced(all_e, 0)
    own = jnp.concatenate([top[:, :HALF], bottom[:, :HALF]], axis=0)
    proj_1 = jnp.concatenate([top[:, HALF:], bottom[:, HALF:]], axis=0)
    reduce_middle(a_l, mid_l, b_l, 3)
    twice_1 = 2.0 * proj_1 - dot3(own, proj_1, NN)
    gram_11 = split_rows(third) - dot3(proj_1, twice_1, TN)
    factor_11, inverse_11 = eliminate(gram_11)
    reduce_last(b_l, sum_l, all_l, 3)
    projected_1 = wide_1 - dot3(proj_1, wide_x, TN)
    basis_1 = dot3(inverse_11, projected_1, NN)
    for v in range(var_count):
        basis_ref[0, v] = basis_1[:, LANES * v:LANES * (v + 1)]

    proj_2, cross, square = [split_rows(x) for x in reduced(all_l, 3)]
    twice_2 = 2.0 * proj_2 - dot3(own, proj_2, NN)
    gram_12 = cross - dot3(twice_1, proj_2, TN)
    gram_22 = square - dot3(proj_2, twice_2, TN)
    factor_12 = dot3(inverse_11, gram_12, NN)
    factor_22, inverse_22 = eliminate(gram_22 - dot3(factor_12, factor_12, TN))
    projected_2 = wide_2 - dot3(proj_2, wide_x, TN) - dot3(factor_12, basis_1, TN)
    basis_2 = dot3(inverse_22, projected_2, NN)
    for v in range(var_count):
        basis_ref[1, v] = basis_2[:, LANES * v:LANES * (v + 1)]
    proj_ref[...] = jnp.concatenate([proj_1, proj_2], axis=1)
    factor_ref[...] = jnp.concatenate([
        jnp.concatenate([factor_11, factor_12], axis=1),
        jnp.concatenate([jnp.zeros((HALF, HALF), F32), factor_22], axis=1),
    ], axis=0)

    wait_edges(edge_out1, ed_send, 0)
    wait_edges(edge_out2, ed_send, 1)
    wait_many(send1, sz.grid - 1, fr_send.at[0])
    wait_many(send2, sz.grid - 1, fr_send.at[1])
    for which, (a_buf, b_buf, all_buf) in ((0, (a_e, b_e, all_e)), (3, (a_l, b_l, all_l))):
        wait_many(a_buf, sz.first - 1, red_send.at[which])
        wait_many(b_buf, sz.low - 1, red_send.at[which + 1])
        wait_many(all_buf, sz.first - 1, red_send.at[which + 2])


def shards(sz, start_block, jacobian, block_cols, donor_cell, donor_weight, fringe_dest, recv_cell):
    var_count, rhs_count, cell_count = start_block.shape
    vmem = pl.BlockSpec(memory_space=pltpu.VMEM)
    smem = pl.BlockSpec(memory_space=pltpu.SMEM)
    field = (var_count, rhs_count, cell_count)
    edge = pltpu.VMEM((2, var_count, PACK, LANES), F32)
    sums = [
        pltpu.VMEM((PACK, 3, LANES), F32),
        pltpu.VMEM((sz.first, sz.share, 3, LANES), F32),
        pltpu.VMEM((sz.share, 3, LANES), F32),
        pltpu.VMEM((sz.low, sz.share, 3, LANES), F32),
        pltpu.VMEM((sz.share, 3, LANES), F32),
        pltpu.VMEM((sz.first, sz.share, 3, LANES), F32),
    ]
    return pl.pallas_call(
        functools.partial(kernel, sz),
        out_shape=(
            jax.ShapeDtypeStruct((2,) + field, F32),
            jax.ShapeDtypeStruct((rhs_count, 2 * rhs_count), F32),
            jax.ShapeDtypeStruct((2 * rhs_count, 2 * rhs_count), F32),
        ),
        in_specs=[smem] + [vmem] * 6,
        out_specs=(vmem, vmem, vmem),
        scratch_shapes=[
            pltpu.VMEM(field, F32),
            pltpu.VMEM(field, F32),
            pltpu.VMEM((4, var_count, 8, LANES), F32),
            pltpu.VMEM((LANES, var_count + 1, LANES), F32),
            pltpu.VMEM((LANES, var_count, LANES), F32),
            pltpu.VMEM((LANES, var_count + 1, LANES), F32),
            pltpu.VMEM((LANES, var_count, LANES), F32),
            pltpu.VMEM((LANES, 2 * LANES), F32),
            pltpu.VMEM((2 * LANES, LANES), BF16),
            edge, edge, edge, edge,
            *sums, *sums,
            pltpu.SemaphoreType.DMA((2,)),
            pltpu.SemaphoreType.DMA((2,)),
            pltpu.SemaphoreType.DMA((4,)),
            pltpu.SemaphoreType.DMA((4,)),
            pltpu.SemaphoreType.DMA((6,)),
            pltpu.SemaphoreType.DMA((6,)),
        ],
        compiler_params=pltpu.CompilerParams(
            collective_id=0, has_side_effects=True, vmem_limit_bytes=32 * 1024 * 1024
        ),
    )(block_cols, start_block, jacobian, donor_cell, donor_weight, fringe_dest,
      recv_cell.reshape(1, recv_cell.shape[0]))


def solution(mesh):
    grid, slab = mesh.shape["grid"], mesh.shape["slab"]
    low = min(16, max(2, grid // 2))
    sz = Sizes(grid, slab, low, 5 * 128 * grid * slab)
    both = ("grid", "slab")
    in_specs = (
        P(None, None, both),
        P(both, None, None, None, None),
        P(both, None),
        P(both, None),
        P(both, None),
        P(both, None),
        P(both),
    )
    out_specs = (P(None, None, None, both), P(), P())
    return jax.shard_map(
        functools.partial(shards, sz), mesh=mesh, in_specs=in_specs, out_specs=out_specs, check_vma=False
    )
```

time: 515 us -> 77.1 us (0.15)
  waiting for transfers between devices: 260 us -> 0 us
  blocking collectives: 99.5 us -> 0 us
  Pallas kernels: 0 us -> 71.9 us
  starting transfers between devices: 53.1 us -> 0 us
  local copies, waits for them, and re-layouts: 39.8 us -> 4.34 us
  other arithmetic: 29.4 us -> 0 us
  matrix products: 17.5 us -> 0 us
  between operations: 14.7 us -> 0.69 us
    psum x1 -> x0, waiting for transfers between devices: 254 us -> none  [shards(): lax.psum(local_gram, ('grid', 'slab')).reshape(2 * rhs_count, 2 * rhs_count)]
    psum x1 -> x0, blocking collectives: 99.5 us -> none  [project_out(): return lax.psum(local_proj, ('grid', 'slab'))]
    pallas_call x0 -> x1, Pallas kernels: none -> 71.9 us  [shards(): pl.pallas_call(functools.partial(kernel, sz), out_shape=(jax.ShapeDtypeSt...]
    all_to_all x3 -> x0, starting transfers between devices: 41.3 us -> none  [the longest x1 18 us: shards(): lax.all_to_all(slot_cells, 'grid', split_axis=1, concat_axis=1, tiled=True)]
    another operation x4 -> x0, other arithmetic: 22.2 us -> none  [the longest x3 12.4 us: upper_factor(): return jnp.linalg.cholesky(gram).T]
    dot_general x16 -> x0, matrix products: 16.3 us -> none  [the longest x8 11 us: apply_blocks(): jnp.einsum('iabc,bric->aric', jacobian[:, column], picked, precision=lax....]
    ppermute x4 -> x0, starting transfers between devices: 11.6 us -> none  [the longest x2 8.89 us: extended(): before = lax.ppermute(last, axis, up)]
    reshape x14 -> x0, local copies, waits for them, and re-layouts: 10.3 us -> none  [the longest x4 4.59 us: apply_blocks(): padded = padded.reshape(var_count, rhs_count, block_count + 2, block_len)]
  transfers between devices with their start and end apart: 8 -> 0, of which waited for: 3 -> 0; matrix products, arithmetic and copies ran while one was open for 9% -> 0% of each run, Pallas kernels for 0% -> 0%
where the time goes in v1:
time: 77.1 us; the launch traced here: 76.9 us
  Pallas kernels  71.9 us (93%)
  local copies, waits for them, and re-layouts  4.34 us (6%)
    pallas_call x1, Pallas kernels, shards(): pl.pallas_call(functools.partial(kernel, sz), out_shape=(jax.ShapeDtypeSt...  71.9 us
    unnamed x19, local copies, waits for them, and re-layouts  4.34 us

profile of v1, /device:TPU:1, one launch (start us, length us, event | category | flops | bytes accessed | tf_op | source)
XLA Modules:
  0.0 76.9 jit_solution(18401061164111916266)
XLA Ops:
  0.6 0.0 copy-start.4
  0.6 0.0 copy-start.3
  0.7 0.8 %copy.11.cell_ref = s32[128,8]{1,0:T(8,128)S(1)} copy(s32[128,8]{0,1:T(8,128)} %param.10) | data formatting | bytes 8192 | tf_op args[3]
  1.5 0.0 copy-done.4
  1.5 0.0 copy-start.5
  1.5 0.1 copy.12.weight_ref
  1.6 0.5 copy-done.5
  2.1 0.0 copy-start
  2.1 0.1 copy.13.dest_ref
  2.3 0.0 copy-done.3
  2.3 0.0 copy-start.1
  2.3 0.0 copy-start.2
  2.3 0.7 copy-done
  3.1 0.0 copy-done.1
  3.1 0.0 copy-done.2
  3.1 71.9 %shard_map.94 = (f32[2,5,64,128]{3,2,1,0:T(8,128)S(1)}, f32[64,128]{1,0:T(8,128)S(1)}, f32[128,128]{1,0:T(8,128)S(1)}) custom-call(s32[2,4]{1,0:T(2,128)S(1)} %copy-done.1, f32[5,64,128]{2,1,0:T(8,128)S(1)} %copy-done, f32[2,4,5,5,64]{4,3,2,1,0:T(8,128)S(1)} %copy.10.jac_ref, s32[128,8]{1,0:T(8,128)S(1)} %copy.11.cell_ref, f32[128,8]{1,0:T(8,128)S(1)} %copy.12.weight_ref, ...), custom_call_target="tpu_custom_call" | custom-call | tf_op jit(solution)/shard_map/pallas_call | solution.py:410
  74.9 0.7 copy.17
  75.7 0.6 copy.18
  76.3 0.6 copy.19
  (1 shorter events, 0.0 us)
Async XLA Ops:
  0.6 0.8 %copy-start.4 = (f32[128,8]{0,1:T(8,128)S(1)}, f32[128,8]{0,1:T(8,128)}, u32[]{:S(2)}) copy-start(f32[128,8]{0,1:T(8,128)} %param.11) | copy-start | bytes 12292
  0.6 1.6 %copy-start.3 = (f32[2,4,5,5,64]{4,1,3,2,0:T(4,128)S(1)}, f32[2,4,5,5,64]{4,1,3,2,0:T(4,128)}, u32[]{:S(2)}) copy-start(f32[2,4,5,5,64]{4,1,3,2,0:T(4,128)} %param.8) | copy-start | bytes 153604
  1.5 0.7 copy-start.5
  2.1 0.9 %copy-start = (f32[5,64,128]{2,1,0:T(8,128)S(1)}, f32[5,64,128]{2,1,0:T(8,128)}, u32[]{:S(2)}) copy-start(f32[5,64,128]{2,1,0:T(8,128)} %x_ref.1) | copy-start | bytes 491524
  2.3 0.8 %copy-start.1 = (s32[2,4]{1,0:T(2,128)S(1)}, s32[2,4]{1,0:T(2,128)}, u32[]{:S(2)}) copy-start(s32[2,4]{1,0:T(2,128)} %cols_ref.1) | copy-start | bytes 100
  2.3 0.8 %copy-start.2 = (s32[128]{0:T(128)S(1)}, s32[128]{0:T(128)}, u32[]{:S(2)}) copy-start(s32[128]{0:T(128)} %param.13) | copy-start | bytes 1540

commit v2 on v1

v2 whole, which is shorter than its diff:
```python
import functools

import jax
import jax.numpy as jnp
from jax import lax
from jax.experimental import pallas as pl
from jax.experimental.pallas import tpu as pltpu
from jax.sharding import PartitionSpec as P

MESH = pl.DeviceIdType.MESH
F32 = jnp.float32
BF16 = jnp.bfloat16
NT = (((1,), (1,)), ((), ()))
NN = (((1,), (0,)), ((), ()))
TN = (((0,), (0,)), ((), ()))
LANES = 128
HALF = 64
PACK = 32
HBM = pltpu.HBM


def halves(x):
    high = x.astype(BF16)
    return high, (x - high.astype(F32)).astype(BF16)


def dot1(a, b, dims):
    return lax.dot_general(a, b, dims, preferred_element_type=F32)


def dot3(a, b, dims):
    ah, al = halves(a)
    bh, bl = halves(b)
    return dot1(ah, bh, dims) + (dot1(ah, bl, dims) + dot1(al, bh, dims))


def lane_ids(shape):
    return lax.broadcasted_iota(jnp.int32, shape, len(shape) - 1)


def row_ids(shape):
    return lax.broadcasted_iota(jnp.int32, shape, len(shape) - 2)


def swap_halves(x):
    return pltpu.roll(x, HALF, x.ndim - 1)


def wide(field):
    return jnp.concatenate([field[v] for v in range(field.shape[0])], axis=1)


def split_rows(packed):
    return jnp.concatenate([packed[:, :HALF], packed[:, HALF:]], axis=0)


def eliminate(gram):
    size = gram.shape[0]
    eye = (row_ids((size, size)) == lane_ids((size, size))).astype(F32)
    work = jnp.concatenate([gram, eye], axis=1)
    blocks = [work[8 * i:8 * i + 8] for i in range(size // 8)]
    sub = row_ids((8, LANES))
    done = []
    for kb in range(len(blocks)):
        cols = {
            i: [jnp.broadcast_to(blocks[i][:, 8 * kb + t:8 * kb + t + 1], (8, LANES)) for t in range(8)]
            for i in range(kb, len(blocks))
        }
        pivots = jnp.ones((8, LANES), F32)
        for t in range(8):
            row = jnp.broadcast_to(blocks[kb][t:t + 1], (8, LANES))
            heads = [jnp.broadcast_to(cols[kb][u][t:t + 1], (8, LANES)) for u in range(t, 8)]
            inverse = 1.0 / heads[0]
            pivots = jnp.where(sub == t, heads[0], pivots)
            for i in range(kb, len(blocks)):
                ratio = cols[i][t] * inverse
                if i == kb:
                    ratio = jnp.where(sub > t, ratio, 0.0)
                for u in range(t + 1, 8):
                    cols[i][u] = cols[i][u] - ratio * heads[u - t]
                blocks[i] = blocks[i] - ratio * row
        done.append(blocks[kb] * lax.rsqrt(pivots))
    both = jnp.concatenate(done, axis=0)
    upper = jnp.where(row_ids((size, size)) <= lane_ids((size, size)), both[:, :size], 0.0)
    return upper, both[:, size:]


class Sizes:
    def __init__(self, ny, nz, nc, ns, total_rows):
        self.ny, self.nz, self.nc, self.ns = ny, nz, nc, ns
        self.grid = ny * nz * nc
        self.first, self.second = nz * ns, ny * nc
        self.share = PACK // self.first
        self.total_rows = total_rows


CHUNKS = ((0,), (1, 2), (3, 4))


def ring(size):
    return sorted(range(size), key=lambda step: -min(step, size - step))


def kernel(sz, *refs):
    (cols_hbm, x_hbm, jac_hbm, cell_hbm, weight_hbm, dest_hbm, recv_hbm,
     basis_ref, proj_ref, factor_ref,
     cols_ref, x_ref, jac_ref, cell_ref, weight_ref, dest_ref, recv_ref, load_sem,
     w1_ref, w2_ref, jeff_ref, place_high, place_low, scatter_ref,
     edge_out1, edge_in1, edge_out2, edge_in2,
     part_e, a_e, mid_e, b_e, sum_e, all_e,
     part_l, a_l, mid_l, b_l, sum_l, all_l,
     fr_send, fr_recv, ed_send, ed_recv, red_send, red_recv, *fringe) = refs
    count = len(CHUNKS)
    send1, got1, send2, got2 = [fringe[k * count:(k + 1) * count] for k in range(4)]
    var_count = x_ref.shape[0]
    g = lax.axis_index("grid")
    s = lax.axis_index("slab")
    core = lax.rem(g, sz.nc)
    z = lax.rem(lax.div(g, sz.nc), sz.nz)
    y = lax.div(g, sz.nc * sz.nz)
    me1 = z * sz.ns + s
    me2 = y * sz.nc + core

    loads = {}
    for k, (name, source, target) in enumerate((
        ("dest", dest_hbm, dest_ref), ("cell", cell_hbm, cell_ref), ("weight", weight_hbm, weight_ref),
        ("recv", recv_hbm, recv_ref), ("x", x_hbm, x_ref), ("jac", jac_hbm, jac_ref), ("cols", cols_hbm, cols_ref),
    )):
        loads[name] = pltpu.make_async_copy(source, target, load_sem.at[k])
        loads[name].start()

    rows_of = [lax.rem(y + step, sz.ny) * (sz.nz * sz.nc) for step in ring(sz.ny)]
    columns_of = [lax.rem(z + step, sz.nz) * sz.nc for step in ring(sz.nz)]
    cores_of = [lax.rem(core + step, sz.nc) for step in ring(sz.nc)]
    slabs_of = [lax.rem(s + step, sz.ns) for step in ring(sz.ns)]
    plane_of = [column + part for column in columns_of for part in cores_of]
    first_of = [(column, slab) for column in columns_of for slab in slabs_of][:-1]
    second_of = [row + part for row in rows_of for part in cores_of][:-1]

    def each_grid_peer(act):
        def body(i, carry):
            row = lax.rem(y + sz.ny // 2 + lax.div(i + 1, 2) * (1 - 2 * lax.rem(i, 2)), sz.ny) * (sz.nz * sz.nc)
            for place in plane_of:
                act(row + place)
            return carry

        lax.fori_loop(0, sz.ny - 1, body, 0)
        for place in plane_of[:-1]:
            act(rows_of[-1] + place)

    if sz.grid < LANES:
        for ref in (*got1, *got2):
            ref[...] = jnp.zeros_like(ref)

    barrier = pltpu.get_barrier_semaphore()

    def greet(p):
        pl.semaphore_signal(barrier, inc=1, device_id=(p, s), device_id_type=MESH)

    each_grid_peer(greet)
    for step in range(1, sz.ns):
        pl.semaphore_signal(barrier, inc=1, device_id=(g, lax.rem(s + step, sz.ns)), device_id_type=MESH)

    rows = dest_ref.shape[1]
    ids = row_ids((LANES, rows))
    for name in ("dest", "cell", "weight", "recv"):
        loads[name].wait()
    named = dest_ref[...] == ids
    later = (row_ids((rows, rows)) < lane_ids((rows, rows))).astype(BF16)
    rank = dot1(named.astype(BF16), later, NN)
    slots = jnp.concatenate(
        [jnp.where(named, (rank == float(j)).astype(F32), 0.0) for j in range(2)], axis=0
    ).astype(BF16)
    weight_mat = jnp.zeros((LANES, rows), F32)
    for t in range(cell_ref.shape[0]):
        weight_mat += jnp.where(cell_ref[t:t + 1, :] == ids, weight_ref[t:t + 1, :], 0.0)
    numbers = jnp.broadcast_to(recv_ref[...].astype(F32) + 1.0, (LANES, rows))
    th, tl = halves(jnp.concatenate([weight_mat, numbers], axis=0))
    placed = dot1(slots, th, NT) + dot1(slots, tl, NT)
    place_high[...], place_low[...] = halves(
        jnp.concatenate([placed[:LANES, :LANES], placed[LANES:, :LANES]], axis=1))
    lanes = lane_ids((LANES, LANES))
    cell_row = jnp.where(lanes < HALF, placed[:LANES, LANES:], placed[LANES:, LANES:])

    def fill_fringe(field_ref, out_ref, chunk):
        zero = jnp.zeros((HALF, LANES), F32)
        blocks = []
        for v in chunk:
            field = field_ref[v]
            blocks += [jnp.concatenate([field, zero], axis=1), jnp.concatenate([zero, field], axis=1)]
        fh, fl = halves(jnp.concatenate(blocks, axis=0))
        ph, plow = place_high[...], place_low[...]
        out = dot1(ph, fh, NT) + (dot1(ph, fl, NT) + dot1(plow, fh, NT))
        for k in range(len(chunk)):
            out_ref[:, k, :] = out[:, LANES * k:LANES * (k + 1)]

    def fill_edges(field_ref, out_ref):
        low_half = lane_ids((PACK, LANES)) < HALF
        for v in range(var_count):
            top, bottom = field_ref[v, :PACK, :], field_ref[v, PACK:, :]
            out_ref[0, v] = jnp.where(low_half, swap_halves(top), bottom)
            out_ref[1, v] = jnp.where(low_half, top, swap_halves(bottom))

    def start_edges(out_ref, in_ref, which):
        for side, step in ((0, 1), (1, sz.ns - 1)):
            pltpu.make_async_remote_copy(
                src_ref=out_ref.at[side], dst_ref=in_ref.at[side],
                send_sem=ed_send.at[2 * which + side], recv_sem=ed_recv.at[2 * which + side],
                device_id=(g, lax.rem(s + step, sz.ns)), device_id_type=MESH,
            ).start()

    def wait_edges(ref, sems, which):
        for side in range(2):
            pltpu.make_async_copy(ref.at[side], ref.at[side], sems.at[2 * which + side]).wait()

    def start_fringe(out_ref, in_ref, which):
        in_ref[g] = out_ref[g]

        def send(p):
            pltpu.make_async_remote_copy(
                src_ref=out_ref.at[p], dst_ref=in_ref.at[g],
                send_sem=fr_send.at[which], recv_sem=fr_recv.at[which],
                device_id=(p, s), device_id_type=MESH,
            ).start()

        each_grid_peer(send)

    def wait_many(ref, number, sem):
        pltpu.make_async_copy(ref.at[pl.ds(0, number)], ref.at[pl.ds(0, number)], sem).wait()

    def own_terms(field_ref, out_ref):
        low_half = lane_ids((HALF, LANES)) < HALF
        for v in range(var_count):
            field = field_ref[v]
            flipped = swap_halves(field)
            left, right = jnp.where(low_half, field, flipped), jnp.where(low_half, flipped, field)
            for a in range(var_count):
                term = jeff_ref[1, a, v:v + 1, :] * left + jeff_ref[2, a, v:v + 1, :] * right
                base = field_ref[a] if v == 0 else out_ref[a]
                out_ref[a] = base + term

    def edge_terms(in_ref, out_ref):
        low_half = lane_ids((PACK, LANES)) < HALF
        for v in range(var_count):
            spread = []
            for side in range(2):
                packed = in_ref[side, v]
                flipped = swap_halves(packed)
                spread.append(jnp.concatenate(
                    [jnp.where(low_half, packed, flipped), jnp.where(low_half, flipped, packed)], axis=0))
            for a in range(var_count):
                term = jeff_ref[0, a, v:v + 1, :] * spread[0] + jeff_ref[3, a, v:v + 1, :] * spread[1]
                out_ref[a] = out_ref[a] + term

    def fringe_terms(in_ref, out_ref, chunk):
        left = []
        for k in range(len(chunk)):
            turned = jnp.transpose(in_ref[:, k, :])
            left.append(jnp.concatenate([turned[:HALF], turned[HALF:]], axis=1))
        lh, ll = halves(jnp.concatenate(left, axis=0))
        scatter = scatter_ref[...]
        total = dot1(lh, scatter, NN) + dot1(ll, scatter, NN)
        for k, v in enumerate(chunk):
            out_ref[v] = out_ref[v] + total[HALF * k:HALF * (k + 1)]

    loads["x"].wait()
    for k, chunk in enumerate(CHUNKS):
        fill_fringe(x_ref, send1[k], chunk)
        if k == 0:
            send1[0][:, len(chunk), :] = cell_row
            pl.semaphore_wait(barrier, sz.grid - 1 + sz.ns - 1)
        start_fringe(send1[k], got1[k], k)
    fill_edges(x_ref, edge_out1)
    start_edges(edge_out1, edge_in1, 0)

    loads["jac"].wait()
    loads["cols"].wait()
    side_on = [(s > 0).astype(F32), F32(1.0), F32(1.0), (s < sz.ns - 1).astype(F32)]
    listed = jac_ref.shape[3]
    low_lane = lane_ids((listed, LANES)) < HALF
    turn = row_ids((listed, LANES))
    picks = []
    for j in range(4):
        pick = jnp.zeros((listed, LANES), F32)
        for k in range(listed):
            left, right = [jnp.where(cols_ref[i, k] == j, side_on[j], F32(0.0)) for i in range(2)]
            pick = jnp.where(turn == k, jnp.where(low_lane, left, right), pick)
        picks.append(pick)
    for a in range(var_count):
        for b in range(var_count):
            both = jnp.concatenate([jac_ref[0, a, b], jac_ref[1, a, b]], axis=1)
            for j in range(4):
                jeff_ref[j, a, b:b + 1, :] = jnp.sum(picks[j] * both, axis=0, keepdims=True)

    own_terms(x_ref, w1_ref)
    wait_edges(edge_in1, ed_recv, 0)
    edge_terms(edge_in1, w1_ref)

    for k, chunk in enumerate(CHUNKS):
        wait_many(got1[k], sz.grid - 1, fr_recv.at[k])
        if k == 0:
            cells = got1[0][:, len(chunk), :]
            numbers = (lanes + 1).astype(F32)
            scatter_ref[...] = jnp.concatenate(
                [(cells[:, j * HALF:j * HALF + 1] == numbers).astype(F32) for j in range(2)], axis=0
            ).astype(BF16)
        fringe_terms(got1[k], w1_ref, chunk)
        fill_fringe(w1_ref, send2[k], chunk)
        start_fringe(send2[k], got2[k], count + k)
    fill_edges(w1_ref, edge_out2)
    start_edges(edge_out2, edge_in2, 1)

    def reduce_start(part, a_buf, which):
        mine = me1 * sz.share
        a_buf[me1] = part[pl.ds(mine, sz.share)]

        for column, slab in first_of:
            q = lax.div(column, sz.nc) * sz.ns + slab
            pltpu.make_async_remote_copy(
                src_ref=part.at[pl.ds(q * sz.share, sz.share)], dst_ref=a_buf.at[me1],
                send_sem=red_send.at[which], recv_sem=red_recv.at[which],
                device_id=(rows_of[-1] + column + core, slab), device_id_type=MESH,
            ).start()

    def reduce_middle(a_buf, mid, b_buf, which):
        wait_many(a_buf, sz.first - 1, red_recv.at[which])
        value = a_buf[0]
        for i in range(1, sz.first):
            value = value + a_buf[i]
        mid[...] = value
        b_buf[me2] = value

        for place in second_of:
            pltpu.make_async_remote_copy(
                src_ref=mid, dst_ref=b_buf.at[me2],
                send_sem=red_send.at[which + 1], recv_sem=red_recv.at[which + 1],
                device_id=(place + columns_of[-1], s), device_id_type=MESH,
            ).start()

    def reduce_last(b_buf, sum_buf, all_buf, which):
        wait_many(b_buf, sz.second - 1, red_recv.at[which + 1])
        value = b_buf[0]
        for i in range(1, sz.second):
            value = value + b_buf[i]
        sum_buf[...] = value
        all_buf[me1] = value

        for column, slab in first_of:
            pltpu.make_async_remote_copy(
                src_ref=sum_buf, dst_ref=all_buf.at[me1],
                send_sem=red_send.at[which + 2], recv_sem=red_recv.at[which + 2],
                device_id=(rows_of[-1] + column + core, slab), device_id_type=MESH,
            ).start()

    def reduced(all_buf, which):
        wait_many(all_buf, sz.first - 1, red_recv.at[which + 2])
        scale = 1.0 / sz.total_rows
        return [all_buf[:, :, t, :].reshape(PACK, LANES) * scale for t in range(3)]

    low_half = lane_ids((PACK, LANES)) < HALF
    wide_x = wide(x_ref)
    wide_1 = wide(w1_ref)
    pair = jnp.concatenate([wide_x, wide_1], axis=0)
    early = dot3(pair, pair, NT)
    part_e[:, 0, :] = early[:PACK]
    part_e[:, 1, :] = early[PACK:HALF]
    part_e[:, 2, :] = jnp.where(low_half, swap_halves(early[HALF:HALF + PACK]), early[HALF + PACK:])
    reduce_start(part_e, a_e, 0)
    own_terms(w1_ref, w2_ref)
    wait_edges(edge_in2, ed_recv, 1)
    edge_terms(edge_in2, w2_ref)
    for k, chunk in enumerate(CHUNKS):
        wait_many(got2[k], sz.grid - 1, fr_recv.at[count + k])
        fringe_terms(got2[k], w2_ref, chunk)

    wide_2 = wide(w2_ref)
    late = dot3(jnp.concatenate([wide_x, wide_1, wide_2], axis=0), wide_2, NT)
    for t in range(3):
        block = late[HALF * t:HALF * (t + 1)]
        part_l[:, t, :] = jnp.concatenate([block[:PACK], block[PACK:]], axis=1)
    reduce_start(part_l, a_l, 3)
    reduce_middle(a_e, mid_e, b_e, 0)
    reduce_middle(a_l, mid_l, b_l, 3)
    reduce_last(b_e, sum_e, all_e, 0)
    reduce_last(b_l, sum_l, all_l, 3)

    top, bottom, third = reduced(all_e, 0)
    own = jnp.concatenate([top[:, :HALF], bottom[:, :HALF]], axis=0)
    proj_1 = jnp.concatenate([top[:, HALF:], bottom[:, HALF:]], axis=0)
    twice_1 = 2.0 * proj_1 - dot3(own, proj_1, NN)
    gram_11 = split_rows(third) - dot3(proj_1, twice_1, TN)
    factor_11, inverse_11 = eliminate(gram_11)
    projected_1 = wide_1 - dot3(proj_1, wide_x, TN)
    basis_1 = dot3(inverse_11, projected_1, NN)
    for v in range(var_count):
        basis_ref[0, v] = basis_1[:, LANES * v:LANES * (v + 1)]

    proj_2, cross, square = [split_rows(value) for value in reduced(all_l, 3)]
    twice_2 = 2.0 * proj_2 - dot3(own, proj_2, NN)
    gram_12 = cross - dot3(twice_1, proj_2, TN)
    gram_22 = square - dot3(proj_2, twice_2, TN)
    factor_12 = dot3(inverse_11, gram_12, NN)
    factor_22, inverse_22 = eliminate(gram_22 - dot3(factor_12, factor_12, TN))
    projected_2 = wide_2 - dot3(proj_2, wide_x, TN) - dot3(factor_12, basis_1, TN)
    basis_2 = dot3(inverse_22, projected_2, NN)
    for v in range(var_count):
        basis_ref[1, v] = basis_2[:, LANES * v:LANES * (v + 1)]
    proj_ref[...] = jnp.concatenate([proj_1, proj_2], axis=1)
    factor_ref[...] = jnp.concatenate([
        jnp.concatenate([factor_11, factor_12], axis=1),
        jnp.concatenate([jnp.zeros((HALF, HALF), F32), factor_22], axis=1),
    ], axis=0)

    wait_edges(edge_out1, ed_send, 0)
    wait_edges(edge_out2, ed_send, 1)
    for k in range(count):
        wait_many(send1[k], sz.grid - 1, fr_send.at[k])
        wait_many(send2[k], sz.grid - 1, fr_send.at[count + k])
    for which, (a_buf, b_buf, all_buf) in ((0, (a_e, b_e, all_e)), (3, (a_l, b_l, all_l))):
        wait_many(a_buf, sz.first - 1, red_send.at[which])
        wait_many(b_buf, sz.second - 1, red_send.at[which + 1])
        wait_many(all_buf, sz.first - 1, red_send.at[which + 2])


def shards(sz, start_block, jacobian, block_cols, donor_cell, donor_weight, fringe_dest, recv_cell):
    var_count, rhs_count, cell_count = start_block.shape
    vmem = pl.BlockSpec(memory_space=pltpu.VMEM)
    field = (var_count, rhs_count, cell_count)
    edge = pltpu.VMEM((2, var_count, PACK, LANES), F32)
    sums = [
        pltpu.VMEM((PACK, 3, LANES), F32),
        pltpu.VMEM((sz.first, sz.share, 3, LANES), F32),
        pltpu.VMEM((sz.share, 3, LANES), F32),
        pltpu.VMEM((sz.second, sz.share, 3, LANES), F32),
        pltpu.VMEM((sz.share, 3, LANES), F32),
        pltpu.VMEM((sz.first, sz.share, 3, LANES), F32),
    ]
    inputs = (
        block_cols,
        start_block,
        jnp.transpose(jacobian, (0, 2, 3, 1, 4)),
        donor_cell.T,
        donor_weight.T,
        fringe_dest.reshape(1, -1),
        recv_cell.reshape(1, -1),
    )
    places = [pltpu.SMEM] + [pltpu.VMEM] * 6
    count = len(CHUNKS)
    first_chunks = [pltpu.VMEM((LANES, len(c) + (k == 0), LANES), F32) for k, c in enumerate(CHUNKS)]
    second_chunks = [pltpu.VMEM((LANES, len(c), LANES), F32) for c in CHUNKS]
    return pl.pallas_call(
        functools.partial(kernel, sz),
        out_shape=(
            jax.ShapeDtypeStruct((2,) + field, F32),
            jax.ShapeDtypeStruct((rhs_count, 2 * rhs_count), F32),
            jax.ShapeDtypeStruct((2 * rhs_count, 2 * rhs_count), F32),
        ),
        in_specs=[pl.BlockSpec(memory_space=HBM)] * 7,
        out_specs=(vmem, vmem, vmem),
        scratch_shapes=[
            *[place(value.shape, value.dtype) for place, value in zip(places, inputs)],
            pltpu.SemaphoreType.DMA((7,)),
            pltpu.VMEM(field, F32),
            pltpu.VMEM(field, F32),
            pltpu.VMEM((4, var_count, 8, LANES), F32),
            pltpu.VMEM((LANES, 2 * LANES), BF16),
            pltpu.VMEM((LANES, 2 * LANES), BF16),
            pltpu.VMEM((2 * LANES, LANES), BF16),
            edge, edge, edge, edge,
            *sums, *sums,
            pltpu.SemaphoreType.DMA((2 * count,)),
            pltpu.SemaphoreType.DMA((2 * count,)),
            pltpu.SemaphoreType.DMA((4,)),
            pltpu.SemaphoreType.DMA((4,)),
            pltpu.SemaphoreType.DMA((6,)),
            pltpu.SemaphoreType.DMA((6,)),
            *first_chunks, *first_chunks, *second_chunks, *second_chunks,
        ],
        compiler_params=pltpu.CompilerParams(
            collective_id=0, has_side_effects=True, vmem_limit_bytes=32 * 1024 * 1024
        ),
    )(*[pltpu.with_memory_space_constraint(value, HBM) for value in inputs])


def solution(mesh):
    grid, slab = mesh.shape["grid"], mesh.shape["slab"]
    side = 8 if grid == 128 else 1
    sz = Sizes(grid // (2 * side), side, 2, slab, 5 * 128 * grid * slab)
    both = ("grid", "slab")
    in_specs = (
        P(None, None, both),
        P(both, None, None, None, None),
        P(both, None),
        P(both, None),
        P(both, None),
        P(both, None),
        P(both),
    )
    out_specs = (P(None, None, None, both), P(), P())
    return jax.shard_map(
        functools.partial(shards, sz), mesh=mesh, in_specs=in_specs, out_specs=out_specs, check_vma=False
    )
```

time: 77.1 us -> 61.5 us (0.80)
  Pallas kernels: 71.9 us -> 58.8 us
  local copies, waits for them, and re-layouts: 4.34 us -> 1.97 us
    pallas_call x1, Pallas kernels: 71.9 us -> 58.8 us  [shards(): pl.pallas_call(functools.partial(kernel, sz), out_shape=(jax.ShapeDtypeSt...]
    unnamed x19 -> x3, local copies, waits for them, and re-layouts: 4.34 us -> 1.97 us
where the time goes in v2:
time: 61.5 us; the launch traced here: 61.4 us
  Pallas kernels  58.8 us (96%)
  local copies, waits for them, and re-layouts  1.97 us (3%)
  between operations  0.64 us (1%)
    pallas_call x1, Pallas kernels, shards(): pl.pallas_call(functools.partial(kernel, sz), out_shape=(jax.ShapeDtypeSt...  58.8 us
    unnamed x3, local copies, waits for them, and re-layouts  1.97 us

profile of v2, /device:TPU:1, one launch (start us, length us, event | category | flops | bytes accessed | tf_op | source)
XLA Modules:
  0.0 61.4 jit_solution(8321809056361089382)
XLA Ops:
  0.6 58.8 %shard_map.94 = (f32[2,5,64,128]{3,2,1,0:T(8,128)S(1)}, f32[64,128]{1,0:T(8,128)S(1)}, f32[128,128]{1,0:T(8,128)S(1)}) custom-call(s32[2,4]{1,0:T(2,128)} %refs_0_.1, f32[5,64,128]{2,1,0:T(8,128)} %refs_1_.1, f32[2,5,5,4,64]{4,3,2,1,0:T(4,128)} %bitcast.5, s32[8,128]{1,0:T(8,128)} %bitcast.6, f32[8,128]{1,0:T(8,128)} %bitcast.7, s32[1,128]{1,0:T(1,128)} %bitcast.8, ...), custom_call_target="tpu_custom_call" | custom-call | tf_op jit(solution)/shard_map/pallas_call | solution.py:451
  59.5 0.7 %copy.13 = f32[2,5,64,128]{3,2,1,0:T(8,128)} copy(f32[2,5,64,128]{3,2,1,0:T(8,128)S(1)} %get-tuple-element.6) | data formatting | bytes 655360
  60.2 0.6 copy.14
  60.8 0.6 %copy.15 = f32[128,128]{1,0:T(8,128)} copy(f32[128,128]{1,0:T(8,128)S(1)} %get-tuple-element.8) | data formatting | bytes 131072

commit v3 on v2

--- a/solution.py
+++ b/solution.py
@@ -105,7 +105,7 @@
     (cols_hbm, x_hbm, jac_hbm, cell_hbm, weight_hbm, dest_hbm, recv_hbm,
      basis_ref, proj_ref, factor_ref,
      cols_ref, x_ref, jac_ref, cell_ref, weight_ref, dest_ref, recv_ref, load_sem,
-     w1_ref, w2_ref, jeff_ref, place_high, place_low, scatter_ref,
+     v_ref, u_ref, jeff_ref, place_high, place_low, scatter_ref,
      edge_out1, edge_in1, edge_out2, edge_in2,
      part_e, a_e, mid_e, b_e, sum_e, all_e,
      part_l, a_l, mid_l, b_l, sum_l, all_l,
@@ -121,6 +121,38 @@
     me1 = z * sz.ns + s
     me2 = y * sz.nc + core
 
+    rows_of = [lax.rem(y + step, sz.ny) * (sz.nz * sz.nc) for step in ring(sz.ny)]
+    columns_of = [lax.rem(z + step, sz.nz) * sz.nc for step in ring(sz.nz)]
+    cores_of = [lax.rem(core + step, sz.nc) for step in ring(sz.nc)]
+    slabs_of = [lax.rem(s + step, sz.ns) for step in ring(sz.ns)]
+    plane_of = [column + part for column in columns_of for part in cores_of]
+    first_of = [(column, slab) for column in columns_of for slab in slabs_of][:-1]
+    second_of = [row + part for row in rows_of for part in cores_of][:-1]
+
+    def each_grid_peer(act):
+        def body(i, carry):
+            row = lax.rem(y + sz.ny // 2 + lax.div(i + 1, 2) * (1 - 2 * lax.rem(i, 2)), sz.ny) * (sz.nz * sz.nc)
+            for place in plane_of:
+                act(row + place)
+            return carry
+
+        lax.fori_loop(0, sz.ny - 1, body, 0)
+        for place in plane_of[:-1]:
+            act(rows_of[-1] + place)
+
+    if sz.grid < LANES:
+        for ref in (*got1, *got2):
+            ref[...] = jnp.zeros_like(ref)
+
+    barrier = pltpu.get_barrier_semaphore()
+
+    def greet(p):
+        pl.semaphore_signal(barrier, inc=1, device_id=(p, s), device_id_type=MESH)
+
+    each_grid_peer(greet)
+    for step in range(1, sz.ns):
+        pl.semaphore_signal(barrier, inc=1, device_id=(g, lax.rem(s + step, sz.ns)), device_id_type=MESH)
+
     loads = {}
     for k, (name, source, target) in enumerate((
         ("dest", dest_hbm, dest_ref), ("cell", cell_hbm, cell_ref), ("weight", weight_hbm, weight_ref),
@@ -128,38 +160,6 @@
     )):
         loads[name] = pltpu.make_async_copy(source, target, load_sem.at[k])
         loads[name].start()
-
-    rows_of = [lax.rem(y + step, sz.ny) * (sz.nz * sz.nc) for step in ring(sz.ny)]
-    columns_of = [lax.rem(z + step, sz.nz) * sz.nc for step in ring(sz.nz)]
-    cores_of = [lax.rem(core + step, sz.nc) for step in ring(sz.nc)]
-    slabs_of = [lax.rem(s + step, sz.ns) for step in ring(sz.ns)]
-    plane_of = [column + part for column in columns_of for part in cores_of]
-    first_of = [(column, slab) for column in columns_of for slab in slabs_of][:-1]
-    second_of = [row + part for row in rows_of for part in cores_of][:-1]
-
-    def each_grid_peer(act):
-        def body(i, carry):
-            row = lax.rem(y + sz.ny // 2 + lax.div(i + 1, 2) * (1 - 2 * lax.rem(i, 2)), sz.ny) * (sz.nz * sz.nc)
-            for place in plane_of:
-                act(row + place)
-            return carry
-
-        lax.fori_loop(0, sz.ny - 1, body, 0)
-        for place in plane_of[:-1]:
-            act(rows_of[-1] + place)
-
-    if sz.grid < LANES:
-        for ref in (*got1, *got2):
-            ref[...] = jnp.zeros_like(ref)
-
-    barrier = pltpu.get_barrier_semaphore()
-
-    def greet(p):
-        pl.semaphore_signal(barrier, inc=1, device_id=(p, s), device_id_type=MESH)
-
-    each_grid_peer(greet)
-    for step in range(1, sz.ns):
-        pl.semaphore_signal(barrier, inc=1, device_id=(g, lax.rem(s + step, sz.ns)), device_id_type=MESH)
 
     rows = dest_ref.shape[1]
     ids = row_ids((LANES, rows))
@@ -236,8 +236,7 @@
             left, right = jnp.where(low_half, field, flipped), jnp.where(low_half, flipped, field)
             for a in range(var_count):
                 term = jeff_ref[1, a, v:v + 1, :] * left + jeff_ref[2, a, v:v + 1, :] * right
-                base = field_ref[a] if v == 0 else out_ref[a]
-                out_ref[a] = base + term
+                out_ref[a] = term if v == 0 else out_ref[a] + term
 
     def edge_terms(in_ref, out_ref):
         low_half = lane_ids((PACK, LANES)) < HALF
@@ -266,11 +265,11 @@
     loads["x"].wait()
     for k, chunk in enumerate(CHUNKS):
         fill_fringe(x_ref, send1[k], chunk)
-        if k == 0:
-            send1[0][:, len(chunk), :] = cell_row
-            pl.semaphore_wait(barrier, sz.grid - 1 + sz.ns - 1)
+    send1[0][:, len(CHUNKS[0]), :] = cell_row
+    fill_edges(x_ref, edge_out1)
+    pl.semaphore_wait(barrier, sz.grid - 1 + sz.ns - 1)
+    for k in range(count):
         start_fringe(send1[k], got1[k], k)
-    fill_edges(x_ref, edge_out1)
     start_edges(edge_out1, edge_in1, 0)
 
     loads["jac"].wait()
@@ -292,9 +291,9 @@
             for j in range(4):
                 jeff_ref[j, a, b:b + 1, :] = jnp.sum(picks[j] * both, axis=0, keepdims=True)
 
-    own_terms(x_ref, w1_ref)
+    own_terms(x_ref, v_ref)
     wait_edges(edge_in1, ed_recv, 0)
-    edge_terms(edge_in1, w1_ref)
+    edge_terms(edge_in1, v_ref)
 
     for k, chunk in enumerate(CHUNKS):
         wait_many(got1[k], sz.grid - 1, fr_recv.at[k])
@@ -304,10 +303,10 @@
             scatter_ref[...] = jnp.concatenate(
                 [(cells[:, j * HALF:j * HALF + 1] == numbers).astype(F32) for j in range(2)], axis=0
             ).astype(BF16)
-        fringe_terms(got1[k], w1_ref, chunk)
-        fill_fringe(w1_ref, send2[k], chunk)
+        fringe_terms(got1[k], v_ref, chunk)
+        fill_fringe(v_ref, send2[k], chunk)
         start_fringe(send2[k], got2[k], count + k)
-    fill_edges(w1_ref, edge_out2)
+    fill_edges(v_ref, edge_out2)
     start_edges(edge_out2, edge_in2, 1)
 
     def reduce_start(part, a_buf, which):
@@ -359,22 +358,22 @@
 
     low_half = lane_ids((PACK, LANES)) < HALF
     wide_x = wide(x_ref)
-    wide_1 = wide(w1_ref)
-    pair = jnp.concatenate([wide_x, wide_1], axis=0)
+    wide_v = wide(v_ref)
+    pair = jnp.concatenate([wide_x, wide_v], axis=0)
     early = dot3(pair, pair, NT)
     part_e[:, 0, :] = early[:PACK]
     part_e[:, 1, :] = early[PACK:HALF]
     part_e[:, 2, :] = jnp.where(low_half, swap_halves(early[HALF:HALF + PACK]), early[HALF + PACK:])
     reduce_start(part_e, a_e, 0)
-    own_terms(w1_ref, w2_ref)
+    own_terms(v_ref, u_ref)
     wait_edges(edge_in2, ed_recv, 1)
-    edge_terms(edge_in2, w2_ref)
+    edge_terms(edge_in2, u_ref)
+    late = jnp.zeros((3 * HALF, HALF), F32)
     for k, chunk in enumerate(CHUNKS):
         wait_many(got2[k], sz.grid - 1, fr_recv.at[count + k])
-        fringe_terms(got2[k], w2_ref, chunk)
-
-    wide_2 = wide(w2_ref)
-    late = dot3(jnp.concatenate([wide_x, wide_1, wide_2], axis=0), wide_2, NT)
+        fringe_terms(got2[k], u_ref, chunk)
+        parts = [jnp.concatenate([ref[v] for v in chunk], axis=1) for ref in (x_ref, v_ref, u_ref)]
+        late = late + dot3(jnp.concatenate(parts, axis=0), parts[2], NT)
     for t in range(3):
         block = late[HALF * t:HALF * (t + 1)]
         part_l[:, t, :] = jnp.concatenate([block[:PACK], block[PACK:]], axis=1)
@@ -386,28 +385,36 @@
 
     top, bottom, third = reduced(all_e, 0)
     own = jnp.concatenate([top[:, :HALF], bottom[:, :HALF]], axis=0)
-    proj_1 = jnp.concatenate([top[:, HALF:], bottom[:, HALF:]], axis=0)
-    twice_1 = 2.0 * proj_1 - dot3(own, proj_1, NN)
-    gram_11 = split_rows(third) - dot3(proj_1, twice_1, TN)
+    with_v = jnp.concatenate([top[:, HALF:], bottom[:, HALF:]], axis=0)
+    eye = (row_ids((HALF, HALF)) == lane_ids((HALF, HALF))).astype(F32)
+    proj_1 = own + with_v
+    lack_1 = eye - proj_1
+    left_1 = with_v + dot3(own, lack_1, NN)
+    gram_11 = split_rows(third) + dot3(
+        jnp.concatenate([with_v, lack_1], axis=0), jnp.concatenate([lack_1, left_1], axis=0), TN)
     factor_11, inverse_11 = eliminate(gram_11)
-    projected_1 = wide_1 - dot3(proj_1, wide_x, TN)
-    basis_1 = dot3(inverse_11, projected_1, NN)
+    wide_u = wide(u_ref)
+    basis_1 = dot3(inverse_11, wide_v + dot3(lack_1, wide_x, TN), NN)
     for v in range(var_count):
         basis_ref[0, v] = basis_1[:, LANES * v:LANES * (v + 1)]
-
-    proj_2, cross, square = [split_rows(value) for value in reduced(all_l, 3)]
-    twice_2 = 2.0 * proj_2 - dot3(own, proj_2, NN)
-    gram_12 = cross - dot3(twice_1, proj_2, TN)
-    gram_22 = square - dot3(proj_2, twice_2, TN)
-    factor_12 = dot3(inverse_11, gram_12, NN)
-    factor_22, inverse_22 = eliminate(gram_22 - dot3(factor_12, factor_12, TN))
-    projected_2 = wide_2 - dot3(proj_2, wide_x, TN) - dot3(factor_12, basis_1, TN)
-    basis_2 = dot3(inverse_22, projected_2, NN)
+    solver = jnp.concatenate(
+        [inverse_11, dot3(inverse_11, left_1, NT), dot3(inverse_11, lack_1, NT)], axis=1)
+
+    with_u, cross, square = [split_rows(value) for value in reduced(all_l, 3)]
+    lack_3 = (own - eye) - with_u
+    left_3 = with_u + dot3(own, lack_3, NN)
+    factor_13 = dot3(solver, jnp.concatenate([cross, lack_3, with_u], axis=0), NN)
+    gram_33 = square + dot3(
+        jnp.concatenate([with_u, lack_3], axis=0), jnp.concatenate([lack_3, left_3], axis=0), TN)
+    factor_22, inverse_22 = eliminate(gram_33 - dot3(factor_13, factor_13, TN))
+    rest = wide_u + dot3(
+        jnp.concatenate([lack_3, -factor_13], axis=0), jnp.concatenate([wide_x, basis_1], axis=0), TN)
+    basis_2 = dot3(inverse_22, rest, NN)
     for v in range(var_count):
         basis_ref[1, v] = basis_2[:, LANES * v:LANES * (v + 1)]
-    proj_ref[...] = jnp.concatenate([proj_1, proj_2], axis=1)
+    proj_ref[...] = jnp.concatenate([proj_1, (proj_1 + with_v) + with_u], axis=1)
     factor_ref[...] = jnp.concatenate([
-        jnp.concatenate([factor_11, factor_12], axis=1),
+        jnp.concatenate([factor_11, 2.0 * factor_11 + factor_13], axis=1),
         jnp.concatenate([jnp.zeros((HALF, HALF), F32), factor_22], axis=1),
     ], axis=0)
 
@@ -420,6 +427,15 @@
         wait_many(a_buf, sz.first - 1, red_send.at[which])
         wait_many(b_buf, sz.second - 1, red_send.at[which + 1])
         wait_many(all_buf, sz.first - 1, red_send.at[which + 2])
+
+
+def write_out(basis_ref, proj_ref, factor_ref, basis_hbm, proj_hbm, factor_hbm, sems):
+    pairs = ((basis_ref, basis_hbm), (proj_ref, proj_hbm), (factor_ref, factor_hbm))
+    copies = [pltpu.make_async_copy(source, target, sems.at[k]) for k, (source, target) in enumerate(pairs)]
+    for copy in copies:
+        copy.start()
+    for copy in copies:
+        copy.wait()
 
 
 def shards(sz, start_block, jacobian, block_cols, donor_cell, donor_weight, fringe_dest, recv_cell):
@@ -448,7 +464,7 @@
     count = len(CHUNKS)
     first_chunks = [pltpu.VMEM((LANES, len(c) + (k == 0), LANES), F32) for k, c in enumerate(CHUNKS)]
     second_chunks = [pltpu.VMEM((LANES, len(c), LANES), F32) for c in CHUNKS]
-    return pl.pallas_call(
+    results = pl.pallas_call(
         functools.partial(kernel, sz),
         out_shape=(
             jax.ShapeDtypeStruct((2,) + field, F32),
@@ -480,6 +496,13 @@
             collective_id=0, has_side_effects=True, vmem_limit_bytes=32 * 1024 * 1024
         ),
     )(*[pltpu.with_memory_space_constraint(value, HBM) for value in inputs])
+    return pl.pallas_call(
+        write_out,
+        out_shape=tuple(jax.ShapeDtypeStruct(value.shape, value.dtype) for value in results),
+        in_specs=[vmem] * 3,
+        out_specs=(pl.BlockSpec(memory_space=HBM),) * 3,
+        scratch_shapes=[pltpu.SemaphoreType.DMA((3,))],
+    )(*results)
 
 
 def solution(mesh):

time: 61.5 us -> 62.9 us (1.023)
  Pallas kernels: 58.8 us -> 60.2 us
    pallas_call x0 -> x1, Pallas kernels: none -> 1.77 us  [shards(): pl.pallas_call(write_out, out_shape=tuple((jax.ShapeDtypeStruct(value.sha...]
    unnamed x3 -> x6, local copies, waits for them, and re-layouts: 1.97 us -> 1.93 us
where the time goes in v3:
time: 62.9 us; the launch traced here: 62.7 us
  Pallas kernels  60.2 us (96%)
  local copies, waits for them, and re-layouts  1.93 us (3%)
  between operations  0.65 us (1%)
    pallas_call x1, Pallas kernels, shards(): pl.pallas_call(functools.partial(kernel, sz), out_shape=(jax.ShapeDtypeSt...  58.4 us
    unnamed x6, local copies, waits for them, and re-layouts  1.93 us
    pallas_call x1, Pallas kernels, shards(): pl.pallas_call(write_out, out_shape=tuple((jax.ShapeDtypeStruct(value.sha...  1.77 us

profile of v3, /device:TPU:1, one launch (start us, length us, event | category | flops | bytes accessed | tf_op | source)
XLA Modules:
  0.0 62.7 jit_solution(16280769862859818874)
XLA Ops:
  0.6 58.4 %shard_map.94 = (f32[2,5,64,128]{3,2,1,0:T(8,128)S(1)}, f32[64,128]{1,0:T(8,128)S(1)}, f32[128,128]{1,0:T(8,128)S(1)}) custom-call(s32[2,4]{1,0:T(2,128)} %refs_0_.1, f32[5,64,128]{2,1,0:T(8,128)} %refs_1_.1, f32[2,5,5,4,64]{4,3,2,1,0:T(4,128)} %bitcast.5, s32[8,128]{1,0:T(8,128)} %bitcast.6, f32[8,128]{1,0:T(8,128)} %bitcast.7, s32[1,128]{1,0:T(1,128)} %bitcast.8, ...), custom_call_target="tpu_custom_call" | custom-call | tf_op jit(solution)/shard_map/pallas_call | solution.py:467
  59.0 0.0 copy-start
  59.1 0.7 %copy-done = f32[2,5,64,128]{3,2,1,0:T(8,128)} copy-done((f32[2,5,64,128]{3,2,1,0:T(8,128)}, f32[2,5,64,128]{3,2,1,0:T(8,128)S(1)}, u32[]{:S(2)}) %copy-start) | copy-done | bytes 327704
  59.8 0.0 copy-start.1
  59.8 0.6 copy-done.1
  60.4 0.0 copy-start.2
  60.4 0.6 copy-done.2
  61.0 1.8 %shard_map.95 = (f32[2,5,64,128]{3,2,1,0:T(8,128)}, f32[64,128]{1,0:T(8,128)}, f32[128,128]{1,0:T(8,128)}) custom-call(f32[2,5,64,128]{3,2,1,0:T(8,128)} %copy-done, f32[64,128]{1,0:T(8,128)} %copy-done.2, f32[128,128]{1,0:T(8,128)} %copy-done.1), custom_call_target="tpu_custom_call" | custom-call | tf_op jit(solution)/shard_map/pallas_call | solution.py:499
Async XLA Ops:
  59.0 0.7 %copy-start = (f32[2,5,64,128]{3,2,1,0:T(8,128)}, f32[2,5,64,128]{3,2,1,0:T(8,128)S(1)}, u32[]{:S(2)}) copy-start(f32[2,5,64,128]{3,2,1,0:T(8,128)S(1)} %get-tuple-element.6.basis_ref) | copy-start | bytes 983044
  59.8 0.6 copy-start.1
  60.4 0.6 copy-start.2

commit v4 on v3

--- a/solution.py
+++ b/solution.py
@@ -502,6 +502,7 @@
         in_specs=[vmem] * 3,
         out_specs=(pl.BlockSpec(memory_space=HBM),) * 3,
         scratch_shapes=[pltpu.SemaphoreType.DMA((3,))],
+        compiler_params=pltpu.CompilerParams(vmem_limit_bytes=2 * 1024 * 1024),
     )(*results)
 
 

time: 62.9 us -> 60 us (0.954)
  local copies, waits for them, and re-layouts: 1.93 us -> 0 us
  Pallas kernels: 60.2 us -> 59.2 us
    unnamed x6 -> x0, local copies, waits for them, and re-layouts: 1.93 us -> none
    pallas_call x1, Pallas kernels: 1.77 us -> 0.78 us  [shards(): pl.pallas_call(write_out, out_shape=tuple((jax.ShapeDtypeStruct(value.sha...]
where the time goes in v4:
time: 60 us; the launch traced here: 59.8 us
  Pallas kernels  59.2 us (99%)
  between operations  0.64 us (1%)
    pallas_call x1, Pallas kernels, shards(): pl.pallas_call(functools.partial(kernel, sz), out_shape=(jax.ShapeDtypeSt...  58.4 us

profile of v4, /device:TPU:1, one launch (start us, length us, event | category | flops | bytes accessed | tf_op | source)
XLA Modules:
  0.0 59.8 jit_solution(5167795203799583688)
XLA Ops:
  0.6 58.4 %shard_map.94 = (f32[2,5,64,128]{3,2,1,0:T(8,128)S(1)}, f32[64,128]{1,0:T(8,128)S(1)}, f32[128,128]{1,0:T(8,128)S(1)}) custom-call(s32[2,4]{1,0:T(2,128)} %refs_0_.1, f32[5,64,128]{2,1,0:T(8,128)} %refs_1_.1, f32[2,5,5,4,64]{4,3,2,1,0:T(4,128)} %bitcast.5, s32[8,128]{1,0:T(8,128)} %bitcast.6, f32[8,128]{1,0:T(8,128)} %bitcast.7, s32[1,128]{1,0:T(1,128)} %bitcast.8, ...), custom_call_target="tpu_custom_call" | custom-call | tf_op jit(solution)/shard_map/pallas_call | solution.py:467
  59.0 0.8 %shard_map.95 = (f32[2,5,64,128]{3,2,1,0:T(8,128)}, f32[64,128]{1,0:T(8,128)}, f32[128,128]{1,0:T(8,128)}) custom-call(f32[2,5,64,128]{3,2,1,0:T(8,128)S(1)} %get-tuple-element.6.basis_ref, f32[64,128]{1,0:T(8,128)S(1)} %get-tuple-element.7.proj_ref, f32[128,128]{1,0:T(8,128)S(1)} %get-tuple-element.8.factor_ref), custom_call_target="tpu_custom_call" | custom-call | tf_op jit(solution)/shard_map/pallas_call | solution.py:499
